TPU v7x, 256 devices: a whole 4x4x8 slice. The times are simulated.
256 devices in a mesh: dp: 16 (over y, z_hi), fsdp: 16 (over x, z_lo, core).
Axes of the slice: x: 4, y: 4, z: 8 (z_hi: 4, z_lo: 2; z = z_hi * 2 + z_lo), core: 2. Of those that a mesh axis runs over, the one named last changes fastest.
Arguments:
- layer_input: bfloat16 [24576, 4096], P('dp', 'fsdp'), may hold values from -6 to 6
- grad_out: bfloat16 [24576, 14336], P('dp', 'fsdp'), may hold values from -0.0546875 to 0.0546875
- subspace: bfloat16 [4096, 1024], P('fsdp'), may hold values from -0.09375 to 0.09375
- up_weight: bfloat16 [16, 896, 4096], P('fsdp', 'dp'), may hold values from -0.09375 to 0.09375
- first_moment: float32 [16, 896, 1024], P('fsdp', 'dp'), may hold values from -4 to 4
- second_moment: float32 [16, 896, 1024], P('fsdp', 'dp'), may hold values from 0.01 to 1
Outputs:
- new_weight: bfloat16 [16, 896, 4096], P(None, 'dp')
- new_first: float32 [16, 896, 1024], P('fsdp', 'dp')
- new_second: float32 [16, 896, 1024], P('fsdp', 'dp')
All inputs are finite; a program needn't handle non-finite values.
Results may differ from a plain program's by a relative error of at most 0.0025.
Values may be sent and summed in bfloat16 or wider, within the bound.
A program may use at most 64 MiB of HBM per device.

v0:
```python
import jax
import jax.numpy as jnp
from jax import lax
from jax.sharding import PartitionSpec as P

beta_one = 0.9
beta_two = 0.999
bias_one = 1.0 - 0.9**10
bias_two = 1.0 - 0.999**10
epsilon = 1e-08
step_size = 0.05


def local(layer_input, grad_out, subspace, up_weight, first_moment, second_moment):
    own_coords = lax.psum_scatter(
        jnp.dot(layer_input, subspace, preferred_element_type=jnp.float32),
        "fsdp",
        scatter_dimension=0,
        tiled=True,
    ).astype(jnp.bfloat16)
    coords = lax.all_gather(own_coords, "fsdp", axis=0, tiled=True)
    projected = lax.psum_scatter(
        lax.dot_general(
            grad_out, coords, (((0,), (0,)), ((), ())), preferred_element_type=jnp.float32
        ),
        "dp",
        scatter_dimension=0,
        tiled=True,
    )
    moment_one = beta_one * first_moment[0] + (1.0 - beta_one) * projected
    moment_two = beta_two * second_moment[0] + (1.0 - beta_two) * projected * projected
    direction = (moment_one / bias_one / (jnp.sqrt(moment_two / bias_two) + epsilon)).astype(
        jnp.bfloat16
    )
    change = lax.dot_general(
        direction,
        lax.all_gather(subspace, "fsdp", axis=0, tiled=True),
        (((1,), (1,)), ((), ())),
        preferred_element_type=jnp.float32,
    )
    updated = (up_weight[0].astype(jnp.float32) - step_size * change).astype(jnp.bfloat16)
    gathered = lax.all_gather(updated[None], "fsdp", axis=0, tiled=True)
    return (gathered, moment_one[None], moment_two[None])


def solution(mesh):
    placed = (
        P("dp", "fsdp"),
        P("dp", "fsdp"),
        P("fsdp", None),
        P("fsdp", "dp", None),
        P("fsdp", "dp", None),
        P("fsdp", "dp", None),
    )
    return jax.shard_map(
        local,
        mesh=mesh,
        in_specs=placed,
        out_specs=(P(None, "dp", None), P("fsdp", "dp", None), P("fsdp", "dp", None)),
        check_vma=False,
    )
```

profile of v0, /device:TPU:1, one launch (start us, length us, event | category | flops | bytes accessed | tf_op | source)
XLA Modules:
  0.0 368.3 jit_solution(8631730578536139675)
XLA Ops:
  7.2 0.0 reduce-scatter.5.cloned.1.call-start
  7.2 5.1 %fusion.16 = f32[1536,1024]{1,0:T(8,128)} fusion(bf16[1536,256]{1,0:T(8,128)(2,1)} %param.6, bf16[256,1024]{1,0:T(8,128)(2,1)} %param.8), kind=kOutput, calls=%fused_computation.20 | convolution fusion | flops 805306368 | bytes 7602176 | tf_op jit(solution)/shard_map/dot_general | solution.py:16
  12.4 0.0 all-gather.5.cloned.1.call-start
  12.4 82.0 %reduce-scatter.5.cloned.1.call-done = f32[96,1024]{1,0:T(8,128)} async-done(((f32[1536,1024]{1,0:T(8,128)}), f32[96,1024]{1,0:T(8,128)}) %reduce-scatter.5.cloned.1.call-update) | async-done | bytes 393232 | tf_op jit(solution)/shard_map/reduce_scatter | solution.py:15
  94.5 1.7 convert_element_type.17
  96.2 0.0 reduce-scatter.7.cloned.1.call-start
  96.2 39.8 %all-gather.5.cloned.1.call-done = bf16[1536,1024]{1,0:T(8,128)(2,1)} async-done(((bf16[96,1024]{1,0:T(8,128)(2,1)}), bf16[1536,1024]{1,0:T(8,128)(2,1)}) %all-gather.5.cloned.1.call-update) | async-done | bytes 3145744 | tf_op jit(solution)/shard_map/all_gather | solution.py:21
  136.0 7.2 %convolution_bitcast_fusion = f32[896,1024]{0,1:T(8,128)} fusion(bf16[1536,1024]{1,0:T(8,128)(2,1)} %all-gather.5.cloned.1.call-done, bf16[1536,896]{1,0:T(8,128)(2,1)S(1)} %copy-done), kind=kOutput, calls=%fused_computation.3 | convolution fusion | flops 2818572288 | bytes 9568256 | tf_op jit(solution)/shard_map/dot_general | solution.py:23
  143.2 5.0 %copy.17 = f32[896,1024]{1,0:T(8,128)} copy(f32[896,1024]{0,1:T(8,128)} %convolution_bitcast_fusion) | data formatting | bytes 7340032
  148.3 0.0 all-gather.7.cloned.1.call-start
  148.3 0.5 all-gather.7.cloned.1.call-update
  148.8 0.0 all-gather.9.cloned.1.call-start
  148.9 0.3 copy-done.1
  149.2 0.2 copy.13
  149.4 2.0 copy.14
  151.3 90.0 %reduce-scatter.7.cloned.1.call-done = f32[56,1024]{1,0:T(8,128)} async-done(((f32[896,1024]{1,0:T(8,128)}), f32[56,1024]{1,0:T(8,128)}) %reduce-scatter.7.cloned.1.call-update) | async-done | bytes 229392
  241.3 1.9 copy.18
  243.3 53.2 %all-gather.7.cloned.1.call-done = bf16[4096,1024]{1,0:T(8,128)(2,1)} async-done(((bf16[256,1024]{1,0:T(8,128)(2,1)}), bf16[4096,1024]{1,0:T(8,128)(2,1)}) %all-gather.7.cloned.1.call-update) | async-done | bytes 8388624 | tf_op jit(solution)/shard_map/all_gather | solution.py:37
  296.5 7.4 %fusion.1 = bf16[56,4096]{1,0:T(8,128)(2,1)} fusion(bf16[4096,1024]{1,0:T(8,128)(2,1)} %all-gather.7.cloned.1.call-done, bf16[1,56,4096]{2,1,0:T(8,128)(2,1)} %param.9, f32[56,1024]{0,1:T(8,128)} %copy.18, f32[1,56,1024]{1,2,0:T(8,128)S(1)} %copy.13, f32[1,56,1024]{1,2,0:T(8,128)} %copy.14), kind=kOutput, calls=%fused_computation.2 | convolution fusion | flops 471367680 | bytes 9994240 | tf_op jit(solution)/shard_map/dot_general | solution.py:35
  303.9 2.3 fusion.7
  306.2 1.9 copy.15
  308.1 1.9 copy.16
  310.1 44.6 %all-gather.9.cloned.1.call-done = bf16[896,4096]{1,0:T(8,128)(2,1)} async-done(((bf16[56,4096]{1,0:T(8,128)(2,1)}), bf16[896,4096]{1,0:T(8,128)(2,1)}) %all-gather.9.cloned.1.call-update) | async-done | bytes 7340048 | tf_op jit(solution)/shard_map/all_gather | solution.py:42
  354.7 7.1 %copy.20 = bf16[16,56,4096]{2,1,0:T(8,128)(2,1)} copy(bf16[16,56,4096]{2,1,0:T(8,128)(2,1)} %bitcast.30) | data formatting | bytes 14680064
  (7 shorter events, 0.1 us)
Async XLA Ops:
  7.2 128.8 %copy-start = (bf16[1536,896]{1,0:T(8,128)(2,1)S(1)}, bf16[1536,896]{1,0:T(8,128)(2,1)}, u32[]{:S(2)}) copy-start(bf16[1536,896]{1,0:T(8,128)(2,1)} %param.7) | copy-start | bytes 8257540
  7.2 87.3 %reduce-scatter.5.cloned.1.call-start = ((), (), s32[]{:S(2)}) async-start(), calls=%async_computation.2 | async-start | bytes 6684672 | tf_op jit(solution)/shard_map/reduce_scatter | solution.py:15
  12.4 123.6 %all-gather.5.cloned.1.call-start = ((), (), s32[]{:S(2)}) async-start(), calls=%async_computation.3 | async-start | bytes 3342336 | tf_op jit(solution)/shard_map/all_gather | solution.py:21
  96.2 145.2 %reduce-scatter.7.cloned.1.call-start = ((), (), s32[]{:S(2)}) async-start(), calls=%async_computation.6 | async-start | bytes 3899392
  148.2 0.9 copy-start.1
  148.3 148.3 %all-gather.7.cloned.1.call-start = ((), (), s32[]{:S(2)}) async-start(), calls=%async_computation.4 | async-start | bytes 8912896 | tf_op jit(solution)/shard_map/all_gather | solution.py:37
  148.8 205.9 %all-gather.9.cloned.1.call-start = ((), (), s32[]{:S(2)}) async-start(), calls=%async_computation.5 | async-start | bytes 7798784 | tf_op jit(solution)/shard_map/all_gather | solution.py:42
Sparse Core Ops, SparseCore 0:
  12.5 81.9 reduce-scatter.4
  96.9 39.0 all-gather.4
  148.4 92.9 reduce-scatter.6
  243.0 53.4 all-gather.6
  304.0 50.6 all-gather.8
where the time goes:
time: 369 us; the launch traced here: 368 us
  waiting for transfers between devices  310 us (84%)
  local copies, waits for them, and re-layouts  20.3 us (6%)
  matrix products  19.7 us (5%)
  between operations  13.8 us (4%)
  other arithmetic  4.02 us (1%)
    unnamed x6, waiting for transfers between devices  90.6 us
    reduce_scatter x1, waiting for transfers between devices, local(): lax.psum_scatter(jnp.dot(layer_input, subspace, preferred_element_type=jn...  82 us
    all_gather x1, waiting for transfers between devices, local(): lax.all_gather(subspace, 'fsdp', axis=0, tiled=True)  53.2 us
    all_gather x1, waiting for transfers between devices, local(): gathered = lax.all_gather(updated[None], 'fsdp', axis=0, tiled=True)  44.6 us
    all_gather x1, waiting for transfers between devices, local(): coords = lax.all_gather(own_coords, 'fsdp', axis=0, tiled=True)  39.8 us
    unnamed x11, local copies, waits for them, and re-layouts  20.3 us
  transfers between devices with their start and end apart: 5, of which 5 were waited for; matrix products, arithmetic and copies ran while one was open for 3% of the time, Pallas kernels for 0%

commit v1 on v0

v1 whole, which is shorter than its diff:
```python
import jax
import jax.numpy as jnp
from jax import lax
from jax.experimental import pallas as pl
from jax.experimental.pallas import tpu as pltpu
from jax.sharding import PartitionSpec as P

beta_one = 0.9
beta_two = 0.999
bias_one = 1.0 - 0.9**10
bias_two = 1.0 - 0.999**10
epsilon = 1e-08
step_size = 0.05

MESH = pl.DeviceIdType.MESH
BF = jnp.bfloat16
F32 = jnp.float32

TOK = 1536
OWN = 96
DIN = 256
R = 1024
HID = 896
UNITS = 56
YROWS = 224
HALF = 512


def body(
    x_hbm, g_hbm, s_hbm, w_hbm, m_ref, v_ref,
    s_out, w_out, d_out, p_out,
    s_all, x_all, g_v, gt, c_all, acc, ysend, yrecv, yown, zrecv, d_own,
    loc, s_ss, s_rs, x_ss, x_rs, c_ss, c_rs, w_ss, w_rs, d_ss, d_rs, y_ss, y_rs, z_ss, z_rs,
):
    dp = lax.axis_index("dp")
    f = lax.axis_index("fsdp")
    y, zh = dp // 4, dp % 4
    x, zl, c = f // 4, (f // 2) % 2, f % 2

    def slot(dx=0, dz=0, dc=0):
        xx = (x + dx) % 4
        zz = (zl + dz) % 2
        cc = (c + dc) % 2
        return xx * 4 + zz * 2 + cc

    def fdev(dx=0, dz=0, dc=0):
        return (dp, slot(dx, dz, dc))

    def ydev(dy):
        return (((y + dy) % 4) * 4 + zh, f)

    def zdev(dz):
        return (y * 4 + (zh + dz) % 4, f)

    pair = fdev(dz=1)
    other = (y * 4 + (zh + 3 + 2 * zl) % 4, slot(dz=1))
    mate = fdev(dc=1)

    load_g = pltpu.make_async_copy(g_hbm, g_v, loc.at[0])
    load_g.start()
    load_s = pltpu.make_async_copy(s_hbm, s_all.at[f], loc.at[1])
    load_s.start()
    load_x = pltpu.make_async_copy(x_hbm.at[pl.ds(f * OWN, OWN)], x_all.at[f], loc.at[2])
    load_x.start()
    load_w = pltpu.make_async_copy(w_hbm, w_out.at[f], loc.at[3])
    load_w.start()

    bar = pltpu.get_barrier_semaphore()

    def greet(k, _):
        pl.semaphore_signal(bar, inc=1, device_id=(dp, (f + k) % 16), device_id_type=MESH)
        return 0

    lax.fori_loop(1, 16, greet, 0)
    for k in (1, 2, 3):
        pl.semaphore_signal(bar, inc=1, device_id=ydev(k), device_id_type=MESH)
        pl.semaphore_signal(bar, inc=1, device_id=zdev(k), device_id_type=MESH)
    pl.semaphore_signal(bar, inc=1, device_id=other, device_id_type=MESH)
    pl.semaphore_wait(bar, 22)

    def send(src, dst, ss, rs, i, to):
        cp = pltpu.make_async_remote_copy(
            src_ref=src, dst_ref=dst, send_sem=ss.at[i], recv_sem=rs.at[i],
            device_id=to, device_id_type=MESH,
        )
        cp.start()
        return cp

    def arrived(dst, ss, rs, i):
        pltpu.make_async_remote_copy(
            src_ref=dst, dst_ref=dst, send_sem=ss.at[i], recv_sem=rs.at[i],
            device_id=mate, device_id_type=MESH,
        ).wait_recv()

    yp = y % 2
    mine = pl.ds(pl.multiple_of(yp * 128, 128), 128)
    mine0 = pl.ds(pl.multiple_of(yp * 128, 64), 64)
    mine1 = pl.ds(pl.multiple_of(yp * 128 + 64, 64), 64)
    his = pl.ds(pl.multiple_of((1 - yp) * 128, 128), 128)
    his0 = pl.ds(pl.multiple_of((1 - yp) * 128, 64), 64)
    his1 = pl.ds(pl.multiple_of((1 - yp) * 128 + 64, 64), 64)
    sent = []

    def s_send(src, dst, i, to):
        sent.append(send(src, dst, s_ss, s_rs, i, to))

    s_send(s_hbm.at[mine0], s_all.at[f, mine0], 0, pair)
    s_send(s_hbm.at[mine1], s_all.at[f, mine1], 1, other)
    for dx in (1, 3, 2):
        s_send(s_hbm.at[mine], s_all.at[f, mine], 1 + dx, fdev(dx=dx))
    s_send(s_hbm, s_all.at[f], 5, mate)

    zs = slot(dz=1)
    arrived(s_all.at[zs, mine0], s_ss, s_rs, 0)
    arrived(s_all.at[zs, mine1], s_ss, s_rs, 1)
    for dx in (1, 3, 2):
        s_send(s_all.at[zs, mine], s_all.at[zs, mine], 5 + dx, fdev(dx=dx))

    def s_forward(q, base):
        s_send(s_all.at[q, mine0], s_all.at[q, mine0], base, ydev(1))
        s_send(s_all.at[q, mine1], s_all.at[q, mine1], base + 1, ydev(3))
        s_send(s_all.at[q, mine], s_all.at[q, mine], base + 2, mate)

    s_forward(zs, 9)

    def x_send(k, _):
        p = (f + k) % 16
        send(x_hbm.at[pl.ds(p * OWN, OWN)], x_all.at[f], x_ss, x_rs, k, (dp, p))
        return 0

    lax.fori_loop(1, 16, x_send, 0)

    load_g.wait()

    def turn(t, _):
        at = pl.ds(pl.multiple_of(t * 128, 128), 128)
        gt[:, at] = g_v[at, :].T
        return 0

    for n, dx in enumerate((1, 3, 2)):
        q = slot(dx=4 - dx)
        arrived(s_all.at[q, mine], s_ss, s_rs, 1 + dx)
        s_forward(q, 12 + 3 * n)
        lax.fori_loop(2 * n, 2 * n + 2, turn, 0)
    for n, dx in enumerate((1, 3, 2)):
        q = slot(dx=4 - dx, dz=1)
        arrived(s_all.at[q, mine], s_ss, s_rs, 5 + dx)
        s_forward(q, 21 + 3 * n)
        lax.fori_loop(6 + 2 * n, 8 + 2 * n, turn, 0)
    forwarded = [(0, 1, 9)]
    forwarded += [(4 - dx, 0, 12 + 3 * n) for n, dx in enumerate((1, 3, 2))]
    forwarded += [(4 - dx, 1, 21 + 3 * n) for n, dx in enumerate((1, 3, 2))]
    for n, (dx, dz, base) in enumerate(forwarded):
        q = slot(dx=dx, dz=dz)
        arrived(s_all.at[q, his0], s_ss, s_rs, base)
        arrived(s_all.at[q, his1], s_ss, s_rs, base + 1)
        s_send(s_all.at[q, his], s_all.at[q, his], 30 + n, mate)
    arrived(s_all.at[slot(dc=1)], s_ss, s_rs, 5)
    for n, (dx, dz, base) in enumerate(forwarded):
        q = slot(dx=dx, dz=dz, dc=1)
        arrived(s_all.at[q, mine], s_ss, s_rs, base + 2)
        arrived(s_all.at[q, his], s_ss, s_rs, 30 + n)

    def x_wait(k, _):
        arrived(x_all.at[(f + 16 - k) % 16], x_ss, x_rs, k)
        return 0

    lax.fori_loop(1, 16, x_wait, 0)
    load_s.wait()
    load_x.wait()
    keep_s = pltpu.make_async_copy(s_all, s_out, loc.at[4])
    keep_s.start()

    acc[...] = jnp.zeros_like(acc)

    def add(i, _):
        acc[...] += jnp.dot(x_all[i], s_all[i], preferred_element_type=F32)
        return 0

    lax.fori_loop(0, 16, add, 0)

    def rows(q):
        return pl.ds(pl.multiple_of(q * OWN, 32), OWN)

    c_all[rows(f), :] = acc[...].astype(BF)

    def gather(own, at, ss, rs):
        done = []

        def go(src, dst, i, to):
            done.append(send(src, dst, ss, rs, i, to))

        def start():
            go(own, at(f), 0, pair)
            for dx in (1, 3, 2):
                go(own, at(f), dx, fdev(dx=dx))
            go(own, at(f), 4, mate)

        def turn_z():
            arrived(at(zs), ss, rs, 0)
            for dx in (1, 3, 2):
                go(at(zs), at(zs), 4 + dx, fdev(dx=dx))
            go(at(zs), at(zs), 8, mate)

        def pass_on():
            for dz, base in ((0, 0), (1, 4)):
                for dx in (1, 3, 2):
                    q = slot(dx=4 - dx, dz=dz)
                    arrived(at(q), ss, rs, base + dx)
                    go(at(q), at(q), 8 + dx + 3 * dz, mate)

        def finish():
            arrived(at(slot(dc=1)), ss, rs, 4)
            arrived(at(slot(dz=1, dc=1)), ss, rs, 8)
            for dz in (0, 1):
                for dx in (1, 3, 2):
                    arrived(at(slot(dx=4 - dx, dz=dz, dc=1)), ss, rs, 8 + dx + 3 * dz)

        def drain():
            for cp in done:
                cp.wait_send()

        return start, turn_z, pass_on, finish, drain

    c_start, c_turn, c_pass, c_finish, c_drain = gather(
        c_all.at[rows(f)], lambda q: c_all.at[rows(q)], c_ss, c_rs
    )
    w_start, w_turn, w_pass, w_finish, w_drain = gather(
        w_hbm, lambda q: w_out.at[q], w_ss, w_rs
    )
    d_start, d_turn, d_pass, d_finish, d_drain = gather(
        d_own, lambda q: d_out.at[q], d_ss, d_rs
    )
    c_start()
    c_turn()
    w_start()
    c_pass()
    c_finish()

    def block(k, h):
        t = (y + k) % 4
        a = gt[pl.ds(pl.multiple_of(t * YROWS, 32), YROWS), :]
        return jnp.dot(a, c_all[:, h * HALF:(h + 1) * HALF], preferred_element_type=F32)

    ysent = []
    for h in range(2):
        for k in (1, 3, 2):
            ysend[h, k - 1] = block(k, h).astype(BF)
            ysent.append(send(ysend.at[h, k - 1], yrecv.at[h, k - 1], y_ss, y_rs, 3 * h + k - 1, ydev(k)))
        yown[h] = block(0, h)
    w_turn()

    zsent = []
    for h in range(2):
        for k in (1, 3, 2):
            arrived(yrecv.at[h, k - 1], y_ss, y_rs, 3 * h + k - 1)
        yown[h] = yown[h] + yrecv[h, 0].astype(F32) + yrecv[h, 1].astype(F32) + yrecv[h, 2].astype(F32)
        for k in (1, 3, 2):
            t = (zh + k) % 4
            src = yown.at[h, pl.ds(pl.multiple_of(t * UNITS, 8), UNITS)]
            zsent.append(send(src, zrecv.at[h, k - 1], z_ss, z_rs, 3 * h + k - 1, zdev(k)))
    for h in range(2):
        cols = slice(h * HALF, (h + 1) * HALF)
        for k in (1, 3, 2):
            arrived(zrecv.at[h, k - 1], z_ss, z_rs, 3 * h + k - 1)
        got = yown[h, pl.ds(pl.multiple_of(zh * UNITS, 8), UNITS), :]
        got = got + zrecv[h, 0] + zrecv[h, 1] + zrecv[h, 2]
        p_out[:, cols] = got
        one = beta_one * m_ref[:, cols] + (1.0 - beta_one) * got
        two = beta_two * v_ref[:, cols] + (1.0 - beta_two) * got * got
        d_own[:, cols] = (one / bias_one / (jnp.sqrt(two / bias_two) + epsilon)).astype(BF)
    keep_d = pltpu.make_async_copy(d_own, d_out.at[f], loc.at[5])
    keep_d.start()
    d_start()
    d_turn()
    w_pass()
    d_pass()
    w_finish()
    d_finish()

    for cp in sent + ysent + zsent:
        cp.wait_send()

    def x_sent(k, _):
        pltpu.make_async_remote_copy(
            src_ref=x_hbm.at[pl.ds(0, OWN)], dst_ref=x_all.at[0], send_sem=x_ss.at[k], recv_sem=x_rs.at[k],
            device_id=mate, device_id_type=MESH,
        ).wait_send()
        return 0

    lax.fori_loop(1, 16, x_sent, 0)
    c_drain()
    w_drain()
    d_drain()
    load_w.wait()
    keep_s.wait()
    keep_d.wait()


def exchange(layer_input, grad_out, subspace, up_weight, first, second):
    hbm = pl.BlockSpec(memory_space=pl.ANY)
    vmem = pl.BlockSpec(memory_space=pltpu.VMEM)
    dma = pltpu.SemaphoreType.DMA
    return pl.pallas_call(
        body,
        out_shape=(
            jax.ShapeDtypeStruct((16, DIN, R), BF),
            jax.ShapeDtypeStruct((16, UNITS, 4096), BF),
            jax.ShapeDtypeStruct((16, UNITS, R), BF),
            jax.ShapeDtypeStruct((UNITS, R), F32),
        ),
        in_specs=[hbm, hbm, hbm, hbm, vmem, vmem],
        out_specs=(hbm, hbm, hbm, vmem),
        scratch_shapes=[
            pltpu.VMEM((16, DIN, R), BF),
            pltpu.VMEM((16, OWN, DIN), BF),
            pltpu.VMEM((TOK, HID), BF),
            pltpu.VMEM((HID, TOK), BF),
            pltpu.VMEM((TOK, R), BF),
            pltpu.VMEM((OWN, R), F32),
            pltpu.VMEM((2, 3, YROWS, HALF), BF),
            pltpu.VMEM((2, 3, YROWS, HALF), BF),
            pltpu.VMEM((2, YROWS, HALF), F32),
            pltpu.VMEM((2, 3, UNITS, HALF), F32),
            pltpu.VMEM((UNITS, R), BF),
            dma((6,)),
            dma((37,)), dma((37,)),
            dma((16,)), dma((16,)),
            dma((15,)), dma((15,)),
            dma((15,)), dma((15,)),
            dma((15,)), dma((15,)),
            dma((6,)), dma((6,)),
            dma((6,)), dma((6,)),
        ],
        compiler_params=pltpu.CompilerParams(
            collective_id=0, has_side_effects=True, vmem_limit_bytes=40 * 2**20
        ),
        cost_estimate=pl.CostEstimate(flops=4 * 10**9, bytes_accessed=4 * 10**7, transcendentals=0),
        name="exchange",
    )(layer_input, grad_out, subspace, up_weight, first, second)


def local(layer_input, grad_out, subspace, up_weight, first_moment, second_moment):
    basis, weights, direction, projected = exchange(
        layer_input, grad_out, subspace, up_weight[0], first_moment[0], second_moment[0]
    )
    moment_one = beta_one * first_moment[0] + (1.0 - beta_one) * projected
    moment_two = beta_two * second_moment[0] + (1.0 - beta_two) * projected * projected
    change = lax.dot_general(
        direction.reshape(HID, R),
        basis.reshape(4096, R),
        (((1,), (1,)), ((), ())),
        preferred_element_type=F32,
    )
    updated = (weights.reshape(HID, 4096).astype(F32) - step_size * change).astype(BF)
    return (updated.reshape(16, UNITS, 4096), moment_one[None], moment_two[None])


def solution(mesh):
    placed = (
        P("dp", "fsdp"),
        P("dp", "fsdp"),
        P("fsdp", None),
        P("fsdp", "dp", None),
        P("fsdp", "dp", None),
        P("fsdp", "dp", None),
    )
    return jax.shard_map(
        local,
        mesh=mesh,
        in_specs=placed,
        out_specs=(P(None, "dp", None), P("fsdp", "dp", None), P("fsdp", "dp", None)),
        check_vma=False,
    )
```

time: 369 us -> 151 us (0.41)
  waiting for transfers between devices: 310 us -> 0 us
  Pallas kernels: 0 us -> 125 us
  between operations: 13.8 us -> 0.66 us
  local copies, waits for them, and re-layouts: 20.3 us -> 9.89 us
  matrix products: 19.7 us -> 14.4 us
    all_gather x3 -> x0, waiting for transfers between devices: 138 us -> none  [the longest x1 53.2 us: local(): lax.all_gather(subspace, 'fsdp', axis=0, tiled=True)]
    pallas_call x0 -> x1, Pallas kernels: none -> 125 us  [exchange(): pl.pallas_call(body, out_shape=(jax.ShapeDtypeStruct((16, DIN, R), BF), j...]
    unnamed x6 -> x0, waiting for transfers between devices: 90.6 us -> none
    reduce_scatter x1 -> x0, waiting for transfers between devices: 82 us -> none  [local(): lax.psum_scatter(jnp.dot(layer_input, subspace, preferred_element_type=jn...]
    unnamed x11 -> x18, local copies, waits for them, and re-layouts: 20.3 us -> 9.89 us
    dot_general x3 -> x1, matrix products: 19.7 us -> 14.4 us  [local(): lax.dot_general(direction.reshape(HID, R), basis.reshape(4096, R), (((1,)...]
  transfers between devices with their start and end apart: 5 -> 0, of which waited for: 5 -> 0; matrix products, arithmetic and copies ran while one was open for 3% -> 0% of each run, Pallas kernels for 0% -> 0%
where the time goes in v1:
time: 151 us; the launch traced here: 150 us
  Pallas kernels  125 us (83%)
  matrix products  14.4 us (10%)
  local copies, waits for them, and re-layouts  9.89 us (7%)
    pallas_call x1, Pallas kernels, exchange(): pl.pallas_call(body, out_shape=(jax.ShapeDtypeStruct((16, DIN, R), BF), j...  125 us
    dot_general x1, matrix products, local(): lax.dot_general(direction.reshape(HID, R), basis.reshape(4096, R), (((1,)...  14.4 us
    unnamed x18, local copies, waits for them, and re-layouts  9.89 us

profile of v1, /device:TPU:1, one launch (start us, length us, event | category | flops | bytes accessed | tf_op | source)
XLA Modules:
  0.0 150.5 jit_solution(6367416837632563069)
XLA Ops:
  0.6 0.0 copy-start
  0.6 0.9 copy-done
  1.6 0.0 copy-start.2
  1.6 0.9 copy-done.2
  2.5 0.0 copy-start.4
  2.5 1.8 %copy-done.4 = bf16[1536,896]{1,0:T(8,128)(2,1)S(1)} copy-done((bf16[1536,896]{1,0:T(8,128)(2,1)S(1)}, bf16[1536,896]{1,0:T(8,128)(2,1)}, u32[]{:S(2)}) %copy-start.4) | copy-done | bytes 2752536
  4.3 0.0 copy-start.5
  4.3 1.1 copy-done.5
  5.4 0.0 copy-start.6
  5.4 1.0 copy-done.6
  6.5 0.0 copy-start.7
  6.5 1.0 copy-done.7
  7.5 124.6 %exchange.1 = (bf16[16,256,1024]{2,1,0:T(8,128)(2,1)}, bf16[16,56,4096]{2,1,0:T(8,128)(2,1)S(1)}, bf16[16,56,1024]{2,1,0:T(8,128)(2,1)S(1)}, f32[56,1024]{1,0:T(8,128)S(1)}) custom-call(bf16[1536,256]{1,0:T(8,128)(2,1)S(1)} %copy-done.5, bf16[1536,896]{1,0:T(8,128)(2,1)S(1)} %copy-done.4, bf16[256,1024]{1,0:T(8,128)(2,1)S(1)} %copy-done.6, ...), custom_call_target="tpu_custom_call" | custom-call | flops 4000000000 | bytes 40000000 | tf_op jit(solution)/shard_map/exchange/pallas_call | solution.py:304
  132.1 0.0 copy-start.8
  132.2 3.0 %copy-done.8 = bf16[16,56,4096]{2,1,0:T(8,128)(2,1)} copy-done((bf16[16,56,4096]{2,1,0:T(8,128)(2,1)}, bf16[16,56,4096]{2,1,0:T(8,128)(2,1)S(1)}, u32[]{:S(2)}) %copy-start.8) | copy-done | bytes 7340056
  135.2 0.0 copy-start.1
  135.2 0.0 copy-start.3
  135.2 14.4 %fusion = bf16[896,4096]{1,0:T(8,128)(2,1)} fusion(bf16[896,4096]{1,0:T(8,128)(2,1)} %bitcast.19, bf16[896,1024]{1,0:T(8,128)(2,1)S(1)} %bitcast.20, bf16[4096,1024]{1,0:T(8,128)(2,1)} %bitcast.21), kind=kOutput, calls=%fused_computation.1 | convolution fusion | flops 7530872832 | bytes 24903680 | tf_op jit(solution)/shard_map/dot_general | solution.py:349
  149.6 0.0 copy-done.1
  149.6 0.0 copy-done.3
  149.6 0.8 fusion.2
Async XLA Ops:
  0.6 0.9 copy-start
  1.6 0.9 copy-start.2
  2.5 1.8 %copy-start.4 = (bf16[1536,896]{1,0:T(8,128)(2,1)S(1)}, bf16[1536,896]{1,0:T(8,128)(2,1)}, u32[]{:S(2)}) copy-start(bf16[1536,896]{1,0:T(8,128)(2,1)} %g_hbm.1) | copy-start | bytes 8257540
  4.3 1.1 copy-start.5
  5.4 1.0 copy-start.6
  6.5 1.0 copy-start.7
  132.1 3.1 %copy-start.8 = (bf16[16,56,4096]{2,1,0:T(8,128)(2,1)}, bf16[16,56,4096]{2,1,0:T(8,128)(2,1)S(1)}, u32[]{:S(2)}) copy-start(bf16[16,56,4096]{2,1,0:T(8,128)(2,1)S(1)} %get-tuple-element.7) | copy-start | bytes 22020100
  135.2 14.4 %copy-start.1 = (f32[1,56,1024]{2,1,0:T(8,128)S(1)}, f32[1,56,1024]{2,1,0:T(8,128)}, u32[]{:S(2)}) copy-start(f32[1,56,1024]{2,1,0:T(8,128)} %param.10) | copy-start | bytes 688132
  135.2 14.4 %copy-start.3 = (f32[1,56,1024]{2,1,0:T(8,128)S(1)}, f32[1,56,1024]{2,1,0:T(8,128)}, u32[]{:S(2)}) copy-start(f32[1,56,1024]{2,1,0:T(8,128)} %param.11) | copy-start | bytes 688132

commit v2 on v1

v2 whole, which is shorter than its diff:
```python
import jax
import jax.numpy as jnp
from jax import lax
from jax.experimental import pallas as pl
from jax.experimental.pallas import tpu as pltpu
from jax.sharding import PartitionSpec as P

beta_one = 0.9
beta_two = 0.999
bias_one = 1.0 - 0.9**10
bias_two = 1.0 - 0.999**10
epsilon = 1e-08
step_size = 0.05

MESH = pl.DeviceIdType.MESH
BF = jnp.bfloat16
F32 = jnp.float32

TOK = 1536
OWN = 96
DIN = 256
R = 1024
HID = 896
UNITS = 56
YROWS = 224
HALF = 512
PARTS = 4
PART = R // PARTS


def body(
    x_hbm, g_hbm, s_hbm, w_hbm, m_hbm, v_hbm,
    s_out, w_out, d_out, p_out,
    s_all, x_all, g_v, gt, c_all, acc, ysend, yrecv, yown, zrecv, d_own, m_ref, v_ref, w_own,
    loc, s_ss, s_rs, x_ss, x_rs, c_ss, c_rs, w_ss, w_rs, d_ss, d_rs, y_ss, y_rs, z_ss, z_rs,
):
    dp = lax.axis_index("dp")
    f = lax.axis_index("fsdp")
    y, zh = dp // 4, dp % 4
    x, zl, c = f // 4, (f // 2) % 2, f % 2

    def slot(dx=0, dz=0, dc=0):
        xx = (x + dx) % 4
        zz = (zl + dz) % 2
        cc = (c + dc) % 2
        return xx * 4 + zz * 2 + cc

    def fdev(dx=0, dz=0, dc=0):
        return (dp, slot(dx, dz, dc))

    def ydev(dy):
        return (((y + dy) % 4) * 4 + zh, f)

    def zdev(dz):
        return (y * 4 + (zh + dz) % 4, f)

    pair = fdev(dz=1)
    other = (y * 4 + (zh + 3 + 2 * zl) % 4, slot(dz=1))
    mate = fdev(dc=1)

    load_g = pltpu.make_async_copy(g_hbm, g_v, loc.at[0])
    load_g.start()
    load_s = pltpu.make_async_copy(s_hbm, s_all.at[f], loc.at[1])
    load_s.start()
    load_x = pltpu.make_async_copy(x_hbm.at[pl.ds(f * OWN, OWN)], x_all.at[f], loc.at[2])
    load_x.start()
    load_w = pltpu.make_async_copy(w_hbm, w_own, loc.at[3])
    load_w.start()

    load_m = pltpu.make_async_copy(m_hbm, m_ref, loc.at[6])
    load_m.start()
    load_v = pltpu.make_async_copy(v_hbm, v_ref, loc.at[7])
    load_v.start()

    bar = pltpu.get_barrier_semaphore()

    def greet(k, _):
        pl.semaphore_signal(bar, inc=1, device_id=(dp, (f + k) % 16), device_id_type=MESH)
        return 0

    lax.fori_loop(1, 16, greet, 0)
    for k in (1, 2, 3):
        pl.semaphore_signal(bar, inc=1, device_id=ydev(k), device_id_type=MESH)
        pl.semaphore_signal(bar, inc=1, device_id=zdev(k), device_id_type=MESH)
    pl.semaphore_signal(bar, inc=1, device_id=other, device_id_type=MESH)
    pl.semaphore_wait(bar, 22)

    def send(src, dst, ss, rs, i, to):
        cp = pltpu.make_async_remote_copy(
            src_ref=src, dst_ref=dst, send_sem=ss.at[i], recv_sem=rs.at[i],
            device_id=to, device_id_type=MESH,
        )
        cp.start()
        return cp

    def arrived(dst, ss, rs, i):
        pltpu.make_async_remote_copy(
            src_ref=dst, dst_ref=dst, send_sem=ss.at[i], recv_sem=rs.at[i],
            device_id=mate, device_id_type=MESH,
        ).wait_recv()

    sent, ysent, zsent = [], [], []
    even = (y + zl) % 2

    def half(e, n=0, size=128):
        return pl.ds(pl.multiple_of(e * 128 + n, 32), size)

    mine, his = half(even), half(1 - even)

    def s_send(src, at, i, to):
        sent.append(send(src, at, s_ss, s_rs, i, to))

    zs = slot(dz=1)
    s_send(s_hbm.at[half(1 - even, 0, 64)], s_all.at[f, half(1 - even, 0, 64)], 0, pair)
    s_send(s_hbm.at[half(1 - even, 64, 64)], s_all.at[f, half(1 - even, 64, 64)], 1, other)
    s_send(s_hbm.at[mine], s_all.at[f, mine], 2, fdev(dx=1))
    s_send(s_hbm.at[mine], s_all.at[f, mine], 3, fdev(dx=3))
    s_send(s_hbm.at[half(even, 64, 32)], s_all.at[f, half(even, 64, 32)], 4, pair)
    s_send(s_hbm.at[half(even, 96, 32)], s_all.at[f, half(even, 96, 32)], 5, other)
    s_send(s_hbm, s_all.at[f], 6, mate)

    arrived(s_all.at[zs, half(even, 0, 64)], s_ss, s_rs, 0)
    arrived(s_all.at[zs, half(even, 64, 64)], s_ss, s_rs, 1)
    s_send(s_all.at[zs, mine], s_all.at[zs, mine], 7, fdev(dx=1))
    s_send(s_all.at[zs, mine], s_all.at[zs, mine], 8, fdev(dx=3))
    s_send(s_all.at[zs, half(even, 0, 32)], s_all.at[zs, half(even, 0, 32)], 9, ydev(1))
    s_send(s_all.at[zs, half(even, 32, 32)], s_all.at[zs, half(even, 32, 32)], 10, ydev(3))
    s_send(s_all.at[zs, mine], s_all.at[zs, mine], 11, mate)

    around = (ydev(1), ydev(3), pair, other)

    def s_around(q, base):
        for n, to in enumerate(around):
            part = half(even, 32 * n, 32)
            s_send(s_all.at[q, part], s_all.at[q, part], base + n, to)
        s_send(s_all.at[q, mine], s_all.at[q, mine], base + 4, mate)

    load_g.wait()

    def turn(t, _):
        at = pl.ds(pl.multiple_of(t * 128, 128), 128)
        gt[:, at] = g_v[at, :].T
        return 0

    by_x = []
    for dz in (0, 1):
        a, b = slot(dx=3, dz=dz), slot(dx=1, dz=dz)
        arrived(s_all.at[a, mine], s_ss, s_rs, 2 + 5 * dz)
        part = half(even, 0, 64)
        s_send(s_all.at[a, part], s_all.at[a, part], 12 + 2 * dz, fdev(dx=1))
        arrived(s_all.at[b, mine], s_ss, s_rs, 3 + 5 * dz)
        part = half(even, 64, 64)
        s_send(s_all.at[b, part], s_all.at[b, part], 13 + 2 * dz, fdev(dx=3))
        s_around(a, 20 + 14 * dz)
        s_around(b, 27 + 14 * dz)
        by_x += [(3, dz, 20 + 14 * dz), (1, dz, 27 + 14 * dz)]
        lax.fori_loop(4 * dz, 4 * dz + 4, turn, 0)

    def x_send(k, _):
        p = (f + k) % 16
        send(x_hbm.at[pl.ds(p * OWN, OWN)], x_all.at[f], x_ss, x_rs, k, (dp, p))
        return 0

    lax.fori_loop(1, 16, x_send, 0)

    for dz in (0, 1):
        q = slot(dx=2, dz=dz)
        arrived(s_all.at[q, half(even, 0, 64)], s_ss, s_rs, 12 + 2 * dz)
        arrived(s_all.at[q, half(even, 64, 64)], s_ss, s_rs, 13 + 2 * dz)
        s_around(q, 48 + 7 * dz)
        by_x += [(2, dz, 48 + 7 * dz)]
    lax.fori_loop(8, 12, turn, 0)

    q = zs
    arrived(s_all.at[q, half(1 - even, 64, 32)], s_ss, s_rs, 4)
    arrived(s_all.at[q, half(1 - even, 96, 32)], s_ss, s_rs, 5)
    arrived(s_all.at[q, half(1 - even, 0, 32)], s_ss, s_rs, 9)
    arrived(s_all.at[q, half(1 - even, 32, 32)], s_ss, s_rs, 10)
    s_send(s_all.at[q, his], s_all.at[q, his], 16, mate)
    base_of = {(dx, dz): base for dx, dz, base in by_x}
    for dx, dz, base in by_x:
        q = slot(dx=dx, dz=dz)
        for n in range(4):
            came = base_of[dx, dz if n < 2 else 1 - dz] + n
            arrived(s_all.at[q, half(1 - even, 32 * n, 32)], s_ss, s_rs, came)
        s_send(s_all.at[q, his], s_all.at[q, his], base + 5, mate)
    arrived(s_all.at[slot(dc=1)], s_ss, s_rs, 6)
    arrived(s_all.at[slot(dz=1, dc=1), mine], s_ss, s_rs, 11)
    arrived(s_all.at[slot(dz=1, dc=1), his], s_ss, s_rs, 16)
    for dx, dz, base in by_x:
        q = slot(dx=dx, dz=dz, dc=1)
        arrived(s_all.at[q, mine], s_ss, s_rs, base + 4)
        arrived(s_all.at[q, his], s_ss, s_rs, base + 5)

    def x_wait(k, _):
        arrived(x_all.at[(f + 16 - k) % 16], x_ss, x_rs, k)
        return 0

    lax.fori_loop(1, 16, x_wait, 0)
    def x_sent(k, _):
        pltpu.make_async_remote_copy(
            src_ref=x_hbm.at[pl.ds(0, OWN)], dst_ref=x_all.at[0], send_sem=x_ss.at[k], recv_sem=x_rs.at[k],
            device_id=mate, device_id_type=MESH,
        ).wait_send()
        return 0

    lax.fori_loop(1, 16, x_sent, 0)
    load_s.wait()
    load_x.wait()
    load_m.wait()
    load_v.wait()
    keep_s = pltpu.make_async_copy(s_all, s_out, loc.at[4])
    keep_s.start()

    acc[...] = jnp.zeros_like(acc)

    def add(i, _):
        acc[...] += jnp.dot(x_all[i], s_all[i], preferred_element_type=F32)
        return 0

    lax.fori_loop(0, 16, add, 0)

    def rows(q):
        return pl.ds(pl.multiple_of(q * OWN, 32), OWN)

    c_all[rows(f), :] = acc[...].astype(BF)

    def gather(own, at, ss, rs):
        done = []

        def go(src, dst, i, to):
            done.append(send(src, dst, ss, rs, i, to))

        def start():
            go(own, at(f), 0, pair)
            go(own, at(f), 1, fdev(dx=1))
            go(own, at(f), 2, fdev(dx=3))
            go(own, at(f), 3, mate)

        def turn_z():
            arrived(at(zs), ss, rs, 0)
            go(at(zs), at(zs), 4, fdev(dx=1))
            go(at(zs), at(zs), 5, fdev(dx=3))
            go(at(zs), at(zs), 6, mate)

        def pass_on(dz):
            base = 7 + 5 * dz
            a, b = slot(dx=3, dz=dz), slot(dx=1, dz=dz)
            arrived(at(a), ss, rs, 1 + 3 * dz)
            go(at(a, 0), at(a, 0), base, fdev(dx=1))
            arrived(at(b), ss, rs, 2 + 3 * dz)
            go(at(b, 1), at(b, 1), base + 1, fdev(dx=3))
            go(at(a), at(a), base + 2, mate)
            go(at(b), at(b), base + 3, mate)

        def pass_last(dz):
            base = 7 + 5 * dz
            q = slot(dx=2, dz=dz)
            arrived(at(q, 0), ss, rs, base)
            arrived(at(q, 1), ss, rs, base + 1)
            go(at(q), at(q), base + 4, mate)

        def finish():
            arrived(at(slot(dc=1)), ss, rs, 3)
            arrived(at(slot(dz=1, dc=1)), ss, rs, 6)
            for dz in (0, 1):
                base = 7 + 5 * dz
                arrived(at(slot(dx=3, dz=dz, dc=1)), ss, rs, base + 2)
                arrived(at(slot(dx=1, dz=dz, dc=1)), ss, rs, base + 3)
                arrived(at(slot(dx=2, dz=dz, dc=1)), ss, rs, base + 4)

        def drain():
            for cp in done:
                cp.wait_send()

        return start, turn_z, pass_on, pass_last, finish, drain

    def w_at(q, part=None):
        if part is None:
            return w_out.at[q]
        return w_out.at[q, :, part * 2048:(part + 1) * 2048]

    def span(h, part):
        if part is None:
            return slice(h * HALF, (h + 1) * HALF)
        return slice(h * HALF + part * HALF // 2, h * HALF + (part + 1) * HALF // 2)

    def c_at(h):
        return lambda q, part=None: c_all.at[rows(q), span(h, part)]

    def d_at(h):
        return lambda q, part=None: d_out.at[q, :, span(h, part)]

    cg = [gather(c_at(h)(f), c_at(h), c_ss.at[h], c_rs.at[h]) for h in range(2)]
    dg = [gather(d_own.at[:, span(h, None)], d_at(h), d_ss.at[h], d_rs.at[h]) for h in range(2)]
    w_start, w_turn, w_pass, w_last, w_finish, w_drain = gather(w_hbm, w_at, w_ss, w_rs)
    START, TURN, PASS, LAST, FINISH, DRAIN = range(6)
    def block(k, p):
        t = (y + k) % 4
        a = gt[pl.ds(pl.multiple_of(t * YROWS, 32), YROWS), :]
        return jnp.dot(a, c_all[:, p * PART:(p + 1) * PART], preferred_element_type=F32)

    def y_start(p):
        for k in (1, 3, 2):
            ysend[p, k - 1] = block(k, p).astype(BF)
            ysent.append(send(ysend.at[p, k - 1], yrecv.at[p, k - 1], y_ss, y_rs, 3 * p + k - 1, ydev(k)))
        yown[p] = block(0, p)

    def z_start(p):
        for k in (1, 3, 2):
            arrived(yrecv.at[p, k - 1], y_ss, y_rs, 3 * p + k - 1)
        yown[p] = yown[p] + yrecv[p, 0].astype(F32) + yrecv[p, 1].astype(F32) + yrecv[p, 2].astype(F32)
        for k in (1, 3, 2):
            t = (zh + k) % 4
            src = yown.at[p, pl.ds(pl.multiple_of(t * UNITS, 8), UNITS)]
            zsent.append(send(src, zrecv.at[p, k - 1], z_ss, z_rs, 3 * p + k - 1, zdev(k)))

    def step(p):
        cols = slice(p * PART, (p + 1) * PART)
        for k in (1, 3, 2):
            arrived(zrecv.at[p, k - 1], z_ss, z_rs, 3 * p + k - 1)
        got = yown[p, pl.ds(pl.multiple_of(zh * UNITS, 8), UNITS), :]
        got = got + zrecv[p, 0] + zrecv[p, 1] + zrecv[p, 2]
        p_out[:, cols] = got
        one = beta_one * m_ref[:, cols] + (1.0 - beta_one) * got
        two = beta_two * v_ref[:, cols] + (1.0 - beta_two) * got * got
        d_own[:, cols] = (one / bias_one / (jnp.sqrt(two / bias_two) + epsilon)).astype(BF)

    c0, c1 = cg
    d0, d1 = dg
    c0[START]()
    c0[TURN]()
    c1[START]()
    c1[TURN]()
    c0[PASS](0)
    c0[PASS](1)
    c0[LAST](0)
    c0[LAST](1)
    c1[PASS](0)
    c1[PASS](1)
    w_start()
    load_w.wait()
    keep_w = pltpu.make_async_copy(w_own, w_out.at[f], loc.at[8])
    keep_w.start()
    c0[FINISH]()
    y_start(0)
    y_start(1)
    c1[LAST](0)
    c1[LAST](1)
    c1[FINISH]()
    y_start(2)
    y_start(3)
    w_turn()
    z_start(0)
    z_start(1)
    w_pass(0)
    z_start(2)
    step(0)
    step(1)
    d0[START]()
    z_start(3)
    d0[TURN]()
    w_pass(1)
    step(2)
    step(3)
    d1[START]()
    d0[PASS](0)
    d0[PASS](1)
    d1[TURN]()
    keep_d = pltpu.make_async_copy(d_own, d_out.at[f], loc.at[5])
    keep_d.start()
    w_last(0)
    d0[LAST](0)
    d0[LAST](1)
    d1[PASS](0)
    d1[PASS](1)
    w_last(1)
    d1[LAST](0)
    d1[LAST](1)
    w_finish()
    d0[FINISH]()
    d1[FINISH]()
    keep_d.wait()
    keep_w.wait()
    w_drain()
    for g in cg + dg:
        g[DRAIN]()
    keep_s.wait()
    for cp in sent + ysent + zsent:
        cp.wait_send()


def exchange(layer_input, grad_out, subspace, up_weight, first, second):
    hbm = pl.BlockSpec(memory_space=pl.ANY)
    vmem = pl.BlockSpec(memory_space=pltpu.VMEM)
    dma = pltpu.SemaphoreType.DMA
    return pl.pallas_call(
        body,
        out_shape=(
            jax.ShapeDtypeStruct((16, DIN, R), BF),
            jax.ShapeDtypeStruct((16, UNITS, 4096), BF),
            jax.ShapeDtypeStruct((16, UNITS, R), BF),
            jax.ShapeDtypeStruct((UNITS, R), F32),
        ),
        in_specs=[hbm] * 6,
        out_specs=(hbm, hbm, hbm, vmem),
        scratch_shapes=[
            pltpu.VMEM((16, DIN, R), BF),
            pltpu.VMEM((16, OWN, DIN), BF),
            pltpu.VMEM((TOK, HID), BF),
            pltpu.VMEM((HID, TOK), BF),
            pltpu.VMEM((TOK, R), BF),
            pltpu.VMEM((OWN, R), F32),
            pltpu.VMEM((PARTS, 3, YROWS, PART), BF),
            pltpu.VMEM((PARTS, 3, YROWS, PART), BF),
            pltpu.VMEM((PARTS, YROWS, PART), F32),
            pltpu.VMEM((PARTS, 3, UNITS, PART), F32),
            pltpu.VMEM((UNITS, R), BF),
            pltpu.VMEM((UNITS, R), F32),
            pltpu.VMEM((UNITS, R), F32),
            pltpu.VMEM((UNITS, 4096), BF),
            dma((9,)),
            dma((62,)), dma((62,)),
            dma((16,)), dma((16,)),
            dma((2, 17)), dma((2, 17)),
            dma((17,)), dma((17,)),
            dma((2, 17)), dma((2, 17)),
            dma((3 * PARTS,)), dma((3 * PARTS,)),
            dma((3 * PARTS,)), dma((3 * PARTS,)),
        ],
        compiler_params=pltpu.CompilerParams(
            collective_id=0, has_side_effects=True, vmem_limit_bytes=60 * 2**20
        ),
        cost_estimate=pl.CostEstimate(flops=4 * 10**9, bytes_accessed=4 * 10**7, transcendentals=0),
        name="exchange",
    )(layer_input, grad_out, subspace, up_weight, first, second)


def finish(d_ref, s_ref, w_ref, p_ref, m_ref, v_ref, o_ref, one_ref, two_ref):
    @pl.when(pl.program_id(0) == 0)
    def _():
        got = p_ref[...]
        one_ref[...] = beta_one * m_ref[...] + (1.0 - beta_one) * got
        two_ref[...] = beta_two * v_ref[...] + (1.0 - beta_two) * got * got

    change = lax.dot_general(
        d_ref[...], s_ref[...], (((1,), (1,)), ((), ())), preferred_element_type=F32
    )
    o_ref[...] = (w_ref[...].astype(F32) - step_size * change).astype(BF)


TILE = 1024


def update(direction, basis, weights, projected, first, second):
    whole = pl.BlockSpec((UNITS, R), lambda i: (0, 0))
    return pl.pallas_call(
        finish,
        grid=(4096 // TILE,),
        out_shape=(
            jax.ShapeDtypeStruct((HID, 4096), BF),
            jax.ShapeDtypeStruct((UNITS, R), F32),
            jax.ShapeDtypeStruct((UNITS, R), F32),
        ),
        in_specs=[
            pl.BlockSpec((HID, R), lambda i: (0, 0)),
            pl.BlockSpec((TILE, R), lambda i: (i, 0)),
            pl.BlockSpec((HID, TILE), lambda i: (0, i)),
            whole, whole, whole,
        ],
        out_specs=(pl.BlockSpec((HID, TILE), lambda i: (0, i)), whole, whole),
        compiler_params=pltpu.CompilerParams(vmem_limit_bytes=60 * 2**20),
        cost_estimate=pl.CostEstimate(flops=8 * 10**9, bytes_accessed=26 * 10**6, transcendentals=0),
        name="update",
    )(direction, basis, weights, projected, first, second)


def local(layer_input, grad_out, subspace, up_weight, first_moment, second_moment):
    basis, weights, direction, projected = exchange(
        layer_input, grad_out, subspace, up_weight[0], first_moment[0], second_moment[0]
    )
    updated, moment_one, moment_two = update(
        direction.reshape(HID, R), basis.reshape(4096, R), weights.reshape(HID, 4096),
        projected, first_moment[0], second_moment[0],
    )
    return (updated.reshape(16, UNITS, 4096), moment_one[None], moment_two[None])


def solution(mesh):
    placed = (
        P("dp", "fsdp"),
        P("dp", "fsdp"),
        P("fsdp", None),
        P("fsdp", "dp", None),
        P("fsdp", "dp", None),
        P("fsdp", "dp", None),
    )
    return jax.shard_map(
        local,
        mesh=mesh,
        in_specs=placed,
        out_specs=(P(None, "dp", None), P("fsdp", "dp", None), P("fsdp", "dp", None)),
        check_vma=False,
    )
```

time: 151 us -> 127 us (0.84)
  matrix products: 14.4 us -> 0 us
  local copies, waits for them, and re-layouts: 9.89 us -> 0 us
    dot_general x1 -> x0, matrix products: 14.4 us -> none  [local(): lax.dot_general(direction.reshape(HID, R), basis.reshape(4096, R), (((1,)...]
    pallas_call x0 -> x1, Pallas kernels: none -> 13.5 us  [update(): pl.pallas_call(finish, grid=(4096 // TILE,), out_shape=(jax.ShapeDtypeStr...]
    pallas_call x1, Pallas kernels: 125 us -> 113 us  [exchange(): pl.pallas_call(body, out_shape=(jax.ShapeDtypeStruct((16, DIN, R), BF), j...]
    unnamed x18 -> x0, local copies, waits for them, and re-layouts: 9.89 us -> none
where the time goes in v2:
time: 127 us
  Pallas kernels  126 us (99%)
    pallas_call x1, Pallas kernels, exchange(): pl.pallas_call(body, out_shape=(jax.ShapeDtypeStruct((16, DIN, R), BF), j...  113 us
    pallas_call x1, Pallas kernels, update(): pl.pallas_call(finish, grid=(4096 // TILE,), out_shape=(jax.ShapeDtypeStr...  13.5 us

profile of v2, /device:TPU:1, one launch (start us, length us, event | category | flops | bytes accessed | tf_op | source)
XLA Modules:
  0.0 127.0 jit_solution(5780581102946541214)
XLA Ops:
  0.6 112.9 %exchange.1 = (bf16[16,256,1024]{2,1,0:T(8,128)(2,1)}, bf16[16,56,4096]{2,1,0:T(8,128)(2,1)}, bf16[16,56,1024]{2,1,0:T(8,128)(2,1)}, f32[56,1024]{1,0:T(8,128)}) custom-call(bf16[1536,256]{1,0:T(8,128)(2,1)} %x_hbm.1, bf16[1536,896]{1,0:T(8,128)(2,1)} %g_hbm.1, bf16[256,1024]{1,0:T(8,128)(2,1)} %s_hbm.1, bf16[56,4096]{1,0:T(8,128)(2,1)} %bitcast.9, ...), custom_call_target="tpu_custom_call" | custom-call | flops 4000000000 | bytes 40000000 | tf_op jit(solution)/shard_map/exchange/pallas_call | solution.py:397
  113.6 13.5 %update.1 = (bf16[896,4096]{1,0:T(8,128)(2,1)}, f32[56,1024]{1,0:T(8,128)}, f32[56,1024]{1,0:T(8,128)}) custom-call(bf16[896,1024]{1,0:T(8,128)(2,1)} %bitcast.17, bf16[4096,1024]{1,0:T(8,128)(2,1)} %bitcast.14, bf16[896,4096]{1,0:T(8,128)(2,1)} %bitcast.16, f32[56,1024]{1,0:T(8,128)} %get-tuple-element.13.p_ref, f32[56,1024]{1,0:T(8,128)} %bitcast.11, ...), custom_call_target="tpu_custom_call" | custom-call | flops 8000000000 | bytes 26000000 | tf_op jit(solution)/shard_map/update/pallas_call | solution.py:457

commit v3 on v2

--- a/solution.py
+++ b/solution.py
@@ -100,130 +100,9 @@
         ).wait_recv()
 
     sent, ysent, zsent = [], [], []
-    even = (y + zl) % 2
-
-    def half(e, n=0, size=128):
-        return pl.ds(pl.multiple_of(e * 128 + n, 32), size)
-
-    mine, his = half(even), half(1 - even)
-
-    def s_send(src, at, i, to):
-        sent.append(send(src, at, s_ss, s_rs, i, to))
-
     zs = slot(dz=1)
-    s_send(s_hbm.at[half(1 - even, 0, 64)], s_all.at[f, half(1 - even, 0, 64)], 0, pair)
-    s_send(s_hbm.at[half(1 - even, 64, 64)], s_all.at[f, half(1 - even, 64, 64)], 1, other)
-    s_send(s_hbm.at[mine], s_all.at[f, mine], 2, fdev(dx=1))
-    s_send(s_hbm.at[mine], s_all.at[f, mine], 3, fdev(dx=3))
-    s_send(s_hbm.at[half(even, 64, 32)], s_all.at[f, half(even, 64, 32)], 4, pair)
-    s_send(s_hbm.at[half(even, 96, 32)], s_all.at[f, half(even, 96, 32)], 5, other)
-    s_send(s_hbm, s_all.at[f], 6, mate)
-
-    arrived(s_all.at[zs, half(even, 0, 64)], s_ss, s_rs, 0)
-    arrived(s_all.at[zs, half(even, 64, 64)], s_ss, s_rs, 1)
-    s_send(s_all.at[zs, mine], s_all.at[zs, mine], 7, fdev(dx=1))
-    s_send(s_all.at[zs, mine], s_all.at[zs, mine], 8, fdev(dx=3))
-    s_send(s_all.at[zs, half(even, 0, 32)], s_all.at[zs, half(even, 0, 32)], 9, ydev(1))
-    s_send(s_all.at[zs, half(even, 32, 32)], s_all.at[zs, half(even, 32, 32)], 10, ydev(3))
-    s_send(s_all.at[zs, mine], s_all.at[zs, mine], 11, mate)
-
-    around = (ydev(1), ydev(3), pair, other)
-
-    def s_around(q, base):
-        for n, to in enumerate(around):
-            part = half(even, 32 * n, 32)
-            s_send(s_all.at[q, part], s_all.at[q, part], base + n, to)
-        s_send(s_all.at[q, mine], s_all.at[q, mine], base + 4, mate)
-
-    load_g.wait()
-
-    def turn(t, _):
-        at = pl.ds(pl.multiple_of(t * 128, 128), 128)
-        gt[:, at] = g_v[at, :].T
-        return 0
-
-    by_x = []
-    for dz in (0, 1):
-        a, b = slot(dx=3, dz=dz), slot(dx=1, dz=dz)
-        arrived(s_all.at[a, mine], s_ss, s_rs, 2 + 5 * dz)
-        part = half(even, 0, 64)
-        s_send(s_all.at[a, part], s_all.at[a, part], 12 + 2 * dz, fdev(dx=1))
-        arrived(s_all.at[b, mine], s_ss, s_rs, 3 + 5 * dz)
-        part = half(even, 64, 64)
-        s_send(s_all.at[b, part], s_all.at[b, part], 13 + 2 * dz, fdev(dx=3))
-        s_around(a, 20 + 14 * dz)
-        s_around(b, 27 + 14 * dz)
-        by_x += [(3, dz, 20 + 14 * dz), (1, dz, 27 + 14 * dz)]
-        lax.fori_loop(4 * dz, 4 * dz + 4, turn, 0)
-
-    def x_send(k, _):
-        p = (f + k) % 16
-        send(x_hbm.at[pl.ds(p * OWN, OWN)], x_all.at[f], x_ss, x_rs, k, (dp, p))
-        return 0
-
-    lax.fori_loop(1, 16, x_send, 0)
-
-    for dz in (0, 1):
-        q = slot(dx=2, dz=dz)
-        arrived(s_all.at[q, half(even, 0, 64)], s_ss, s_rs, 12 + 2 * dz)
-        arrived(s_all.at[q, half(even, 64, 64)], s_ss, s_rs, 13 + 2 * dz)
-        s_around(q, 48 + 7 * dz)
-        by_x += [(2, dz, 48 + 7 * dz)]
-    lax.fori_loop(8, 12, turn, 0)
-
-    q = zs
-    arrived(s_all.at[q, half(1 - even, 64, 32)], s_ss, s_rs, 4)
-    arrived(s_all.at[q, half(1 - even, 96, 32)], s_ss, s_rs, 5)
-    arrived(s_all.at[q, half(1 - even, 0, 32)], s_ss, s_rs, 9)
-    arrived(s_all.at[q, half(1 - even, 32, 32)], s_ss, s_rs, 10)
-    s_send(s_all.at[q, his], s_all.at[q, his], 16, mate)
-    base_of = {(dx, dz): base for dx, dz, base in by_x}
-    for dx, dz, base in by_x:
-        q = slot(dx=dx, dz=dz)
-        for n in range(4):
-            came = base_of[dx, dz if n < 2 else 1 - dz] + n
-            arrived(s_all.at[q, half(1 - even, 32 * n, 32)], s_ss, s_rs, came)
-        s_send(s_all.at[q, his], s_all.at[q, his], base + 5, mate)
-    arrived(s_all.at[slot(dc=1)], s_ss, s_rs, 6)
-    arrived(s_all.at[slot(dz=1, dc=1), mine], s_ss, s_rs, 11)
-    arrived(s_all.at[slot(dz=1, dc=1), his], s_ss, s_rs, 16)
-    for dx, dz, base in by_x:
-        q = slot(dx=dx, dz=dz, dc=1)
-        arrived(s_all.at[q, mine], s_ss, s_rs, base + 4)
-        arrived(s_all.at[q, his], s_ss, s_rs, base + 5)
-
-    def x_wait(k, _):
-        arrived(x_all.at[(f + 16 - k) % 16], x_ss, x_rs, k)
-        return 0
-
-    lax.fori_loop(1, 16, x_wait, 0)
-    def x_sent(k, _):
-        pltpu.make_async_remote_copy(
-            src_ref=x_hbm.at[pl.ds(0, OWN)], dst_ref=x_all.at[0], send_sem=x_ss.at[k], recv_sem=x_rs.at[k],
-            device_id=mate, device_id_type=MESH,
-        ).wait_send()
-        return 0
-
-    lax.fori_loop(1, 16, x_sent, 0)
-    load_s.wait()
-    load_x.wait()
-    load_m.wait()
-    load_v.wait()
-    keep_s = pltpu.make_async_copy(s_all, s_out, loc.at[4])
-    keep_s.start()
-
-    acc[...] = jnp.zeros_like(acc)
-
-    def add(i, _):
-        acc[...] += jnp.dot(x_all[i], s_all[i], preferred_element_type=F32)
-        return 0
-
-    lax.fori_loop(0, 16, add, 0)
-
     def rows(q):
         return pl.ds(pl.multiple_of(q * OWN, 32), OWN)
-
-    c_all[rows(f), :] = acc[...].astype(BF)
 
     def gather(own, at, ss, rs):
         done = []
@@ -295,6 +174,122 @@
     dg = [gather(d_own.at[:, span(h, None)], d_at(h), d_ss.at[h], d_rs.at[h]) for h in range(2)]
     w_start, w_turn, w_pass, w_last, w_finish, w_drain = gather(w_hbm, w_at, w_ss, w_rs)
     START, TURN, PASS, LAST, FINISH, DRAIN = range(6)
+    own_class = (y + 2 * zl) % 4
+
+    def rows4(off, n=None):
+        base = ((own_class + off) % 4) * 64
+        if n is None:
+            return pl.ds(pl.multiple_of(base, 64), 64)
+        return pl.ds(pl.multiple_of(base + 32 * n, 32), 32)
+
+    mine = rows4(0)
+
+    def s_send(src, at, i, to):
+        sent.append(send(src, at, s_ss, s_rs, i, to))
+
+    for n, to in enumerate((pair, other)):
+        s_send(s_hbm.at[rows4(2, n)], s_all.at[f, rows4(2, n)], n, to)
+    s_send(s_hbm.at[mine], s_all.at[f, mine], 2, fdev(dx=1))
+    s_send(s_hbm.at[mine], s_all.at[f, mine], 3, fdev(dx=3))
+    for n, to in enumerate((pair, other)):
+        s_send(s_hbm.at[rows4(0, n)], s_all.at[f, rows4(0, n)], 4 + n, to)
+    s_send(s_hbm, s_all.at[f], 6, mate)
+
+    for n in range(2):
+        arrived(s_all.at[zs, rows4(0, n)], s_ss, s_rs, n)
+    s_send(s_all.at[zs, mine], s_all.at[zs, mine], 7, fdev(dx=1))
+    s_send(s_all.at[zs, mine], s_all.at[zs, mine], 8, fdev(dx=3))
+    s_send(s_all.at[zs, mine], s_all.at[zs, mine], 9, ydev(1))
+    s_send(s_all.at[zs, mine], s_all.at[zs, mine], 10, ydev(3))
+
+    def s_around(q, base):
+        s_send(s_all.at[q, mine], s_all.at[q, mine], base, ydev(1))
+        s_send(s_all.at[q, mine], s_all.at[q, mine], base + 1, ydev(3))
+        s_send(s_all.at[q, rows4(0, 0)], s_all.at[q, rows4(0, 0)], base + 2, pair)
+        s_send(s_all.at[q, rows4(0, 1)], s_all.at[q, rows4(0, 1)], base + 3, other)
+
+    load_g.wait()
+
+    def turn(t, _):
+        at = pl.ds(pl.multiple_of(t * 128, 128), 128)
+        gt[:, at] = g_v[at, :].T
+        return 0
+
+    by_x = []
+    for dz in (0, 1):
+        a, b = slot(dx=3, dz=dz), slot(dx=1, dz=dz)
+        arrived(s_all.at[a, mine], s_ss, s_rs, 2 + 5 * dz)
+        s_send(s_all.at[a, rows4(0, 0)], s_all.at[a, rows4(0, 0)], 12 + 2 * dz, fdev(dx=1))
+        arrived(s_all.at[b, mine], s_ss, s_rs, 3 + 5 * dz)
+        s_send(s_all.at[b, rows4(0, 1)], s_all.at[b, rows4(0, 1)], 13 + 2 * dz, fdev(dx=3))
+        s_around(a, 20 + 10 * dz)
+        s_around(b, 25 + 10 * dz)
+        by_x += [(3, dz, 20 + 10 * dz), (1, dz, 25 + 10 * dz)]
+
+    def x_send(k, _):
+        p = (f + k) % 16
+        send(x_hbm.at[pl.ds(p * OWN, OWN)], x_all.at[f], x_ss, x_rs, k, (dp, p))
+        return 0
+
+    lax.fori_loop(1, 16, x_send, 0)
+
+    for dz in (0, 1):
+        q = slot(dx=2, dz=dz)
+        arrived(s_all.at[q, rows4(0, 0)], s_ss, s_rs, 12 + 2 * dz)
+        arrived(s_all.at[q, rows4(0, 1)], s_ss, s_rs, 13 + 2 * dz)
+        s_around(q, 40 + 5 * dz)
+        by_x += [(2, dz, 40 + 5 * dz)]
+    lax.fori_loop(0, 12, turn, 0)
+
+    arrived(s_all.at[zs, rows4(2, 0)], s_ss, s_rs, 4)
+    arrived(s_all.at[zs, rows4(2, 1)], s_ss, s_rs, 5)
+    arrived(s_all.at[zs, rows4(3)], s_ss, s_rs, 9)
+    arrived(s_all.at[zs, rows4(1)], s_ss, s_rs, 10)
+    s_send(s_all.at[zs], s_all.at[zs], 11, mate)
+    base_of = {(dx, dz): base for dx, dz, base in by_x}
+    for dx, dz, base in by_x:
+        q = slot(dx=dx, dz=dz)
+        arrived(s_all.at[q, rows4(3)], s_ss, s_rs, base)
+        arrived(s_all.at[q, rows4(1)], s_ss, s_rs, base + 1)
+        came = base_of[dx, 1 - dz]
+        arrived(s_all.at[q, rows4(2, 0)], s_ss, s_rs, came + 2)
+        arrived(s_all.at[q, rows4(2, 1)], s_ss, s_rs, came + 3)
+        s_send(s_all.at[q], s_all.at[q], base + 4, mate)
+    arrived(s_all.at[slot(dc=1)], s_ss, s_rs, 6)
+    arrived(s_all.at[slot(dz=1, dc=1)], s_ss, s_rs, 11)
+    for dx, dz, base in by_x:
+        arrived(s_all.at[slot(dx=dx, dz=dz, dc=1)], s_ss, s_rs, base + 4)
+
+    def x_wait(k, _):
+        arrived(x_all.at[(f + 16 - k) % 16], x_ss, x_rs, k)
+        return 0
+
+    lax.fori_loop(1, 16, x_wait, 0)
+    def x_sent(k, _):
+        pltpu.make_async_remote_copy(
+            src_ref=x_hbm.at[pl.ds(0, OWN)], dst_ref=x_all.at[0], send_sem=x_ss.at[k], recv_sem=x_rs.at[k],
+            device_id=mate, device_id_type=MESH,
+        ).wait_send()
+        return 0
+
+    lax.fori_loop(1, 16, x_sent, 0)
+    load_s.wait()
+    load_x.wait()
+    load_m.wait()
+    load_v.wait()
+    keep_s = pltpu.make_async_copy(s_all, s_out, loc.at[4])
+    keep_s.start()
+
+    acc[...] = jnp.zeros_like(acc)
+
+    def add(i, _):
+        acc[...] += jnp.dot(x_all[i], s_all[i], preferred_element_type=F32)
+        return 0
+
+    lax.fori_loop(0, 16, add, 0)
+
+    c_all[rows(f), :] = acc[...].astype(BF)
+
     def block(k, p):
         t = (y + k) % 4
         a = gt[pl.ds(pl.multiple_of(t * YROWS, 32), YROWS), :]
@@ -420,7 +415,7 @@
             pltpu.VMEM((UNITS, R), F32),
             pltpu.VMEM((UNITS, 4096), BF),
             dma((9,)),
-            dma((62,)), dma((62,)),
+            dma((50,)), dma((50,)),
             dma((16,)), dma((16,)),
             dma((2, 17)), dma((2, 17)),
             dma((17,)), dma((17,)),

time: 127 us -> 121 us (0.953)
  Pallas kernels: 126 us -> 120 us
    pallas_call x1, Pallas kernels: 113 us -> 107 us  [exchange(): pl.pallas_call(body, out_shape=(jax.ShapeDtypeStruct((16, DIN, R), BF), j...]
where the time goes in v3:
time: 121 us
  Pallas kernels  120 us (99%)
    pallas_call x1, Pallas kernels, exchange(): pl.pallas_call(body, out_shape=(jax.ShapeDtypeStruct((16, DIN, R), BF), j...  107 us
    pallas_call x1, Pallas kernels, update(): pl.pallas_call(finish, grid=(4096 // TILE,), out_shape=(jax.ShapeDtypeStr...  13.5 us

profile of v3, /device:TPU:1, one launch (start us, length us, event | category | flops | bytes accessed | tf_op | source)
XLA Modules:
  0.0 121.0 jit_solution(6948292190426636850)
XLA Ops:
  0.6 106.9 %exchange.1 = (bf16[16,256,1024]{2,1,0:T(8,128)(2,1)}, bf16[16,56,4096]{2,1,0:T(8,128)(2,1)}, bf16[16,56,1024]{2,1,0:T(8,128)(2,1)}, f32[56,1024]{1,0:T(8,128)}) custom-call(bf16[1536,256]{1,0:T(8,128)(2,1)} %x_hbm.1, bf16[1536,896]{1,0:T(8,128)(2,1)} %g_hbm.1, bf16[256,1024]{1,0:T(8,128)(2,1)} %s_hbm.1, bf16[56,4096]{1,0:T(8,128)(2,1)} %bitcast.9, ...), custom_call_target="tpu_custom_call" | custom-call | flops 4000000000 | bytes 40000000 | tf_op jit(solution)/shard_map/exchange/pallas_call | solution.py:392
  107.5 13.5 %update.1 = (bf16[896,4096]{1,0:T(8,128)(2,1)}, f32[56,1024]{1,0:T(8,128)}, f32[56,1024]{1,0:T(8,128)}) custom-call(bf16[896,1024]{1,0:T(8,128)(2,1)} %bitcast.17, bf16[4096,1024]{1,0:T(8,128)(2,1)} %bitcast.14, bf16[896,4096]{1,0:T(8,128)(2,1)} %bitcast.16, f32[56,1024]{1,0:T(8,128)} %get-tuple-element.13.p_ref, f32[56,1024]{1,0:T(8,128)} %bitcast.11, ...), custom_call_target="tpu_custom_call" | custom-call | flops 8000000000 | bytes 26000000 | tf_op jit(solution)/shard_map/update/pallas_call | solution.py:452

commit v4 on v3

--- a/solution.py
+++ b/solution.py
@@ -299,6 +299,8 @@
         for k in (1, 3, 2):
             ysend[p, k - 1] = block(k, p).astype(BF)
             ysent.append(send(ysend.at[p, k - 1], yrecv.at[p, k - 1], y_ss, y_rs, 3 * p + k - 1, ydev(k)))
+
+    def y_own(p):
         yown[p] = block(0, p)
 
     def z_start(p):
@@ -340,12 +342,16 @@
     c0[FINISH]()
     y_start(0)
     y_start(1)
+    y_own(0)
+    y_own(1)
     c1[LAST](0)
     c1[LAST](1)
     c1[FINISH]()
     y_start(2)
     y_start(3)
     w_turn()
+    y_own(2)
+    y_own(3)
     z_start(0)
     z_start(1)
     w_pass(0)

time: 121 us -> 121 us (level)
  no operation moved by 1% of the time
where the time goes in v4:
time: 121 us
  Pallas kernels  121 us (100%)
    pallas_call x1, Pallas kernels, exchange(): pl.pallas_call(body, out_shape=(jax.ShapeDtypeStruct((16, DIN, R), BF), j...  107 us
    pallas_call x1, Pallas kernels, update(): pl.pallas_call(finish, grid=(4096 // TILE,), out_shape=(jax.ShapeDtypeStr...  13.5 us

profile of v4, /device:TPU:1, one launch (start us, length us, event | category | flops | bytes accessed | tf_op | source)
XLA Modules:
  0.0 121.2 jit_solution(11040904436888253142)
XLA Ops:
  0.6 107.1 %exchange.1 = (bf16[16,256,1024]{2,1,0:T(8,128)(2,1)}, bf16[16,56,4096]{2,1,0:T(8,128)(2,1)}, bf16[16,56,1024]{2,1,0:T(8,128)(2,1)}, f32[56,1024]{1,0:T(8,128)}) custom-call(bf16[1536,256]{1,0:T(8,128)(2,1)} %x_hbm.1, bf16[1536,896]{1,0:T(8,128)(2,1)} %g_hbm.1, bf16[256,1024]{1,0:T(8,128)(2,1)} %s_hbm.1, bf16[56,4096]{1,0:T(8,128)(2,1)} %bitcast.9, ...), custom_call_target="tpu_custom_call" | custom-call | flops 4000000000 | bytes 40000000 | tf_op jit(solution)/shard_map/exchange/pallas_call | solution.py:398
  107.8 13.5 %update.1 = (bf16[896,4096]{1,0:T(8,128)(2,1)}, f32[56,1024]{1,0:T(8,128)}, f32[56,1024]{1,0:T(8,128)}) custom-call(bf16[896,1024]{1,0:T(8,128)(2,1)} %bitcast.17, bf16[4096,1024]{1,0:T(8,128)(2,1)} %bitcast.14, bf16[896,4096]{1,0:T(8,128)(2,1)} %bitcast.16, f32[56,1024]{1,0:T(8,128)} %get-tuple-element.13.p_ref, f32[56,1024]{1,0:T(8,128)} %bitcast.11, ...), custom_call_target="tpu_custom_call" | custom-call | flops 8000000000 | bytes 26000000 | tf_op jit(solution)/shard_map/update/pallas_call | solution.py:458
